TPU v7x, 1024 devices: a whole 4x8x16 slice. The times are simulated.
1024 devices in a mesh: mp: 2 (over y_lo), row: 16 (over y_hi, x), col: 32 (over z, core).
Axes of the slice: x: 4, y: 8 (y_hi: 4, y_lo: 2; y = y_hi * 2 + y_lo), z: 16, core: 2. Of those that a mesh axis runs over, the one named last changes fastest.
Arguments:
- text_embeds: bfloat16 [160, 8192], P('row', 'col'), may hold values from -6 to 6
- image_embeds: bfloat16 [64, 8192], P(('mp', 'row'), 'col'), may hold values from -6 to 6
- offsets: int32 [4], replicated, may hold values from 0 to 16, as said below
- lengths: int32 [4], replicated, may hold values from 32 to 40
- loss_mask: int32 [160], P('row'), may hold values 0 or 1
- norm_gain: bfloat16 [2, 8192], P('mp', 'col'), may hold values from 0.5 to 1.5
- unembed_rows: bfloat16 [2, 160, 8192], P('mp', 'row', 'col'), may hold values from -0.0625 to 0.0625
- gate_up: bfloat16 [2, 8192, 2, 29568], P('mp', 'col', None, 'row'), may hold values from -0.0625 to 0.0625
- down_proj: bfloat16 [2, 29568, 8192], P('mp', 'row', 'col'), may hold values from -0.03125 to 0.03125
Outputs:
- dpo_loss: float32 [], replicated
- input_grad: float32 [160, 8192], P(('mp', 'row'), 'col')
Inputs may be any that keep to these rules, and one draw needn't show every extreme that they name: Each sequence's image tokens end at least 8 positions before its end: offsets[s] + 24 <= 40. Tokens at or after lengths[s] are padding and never scored.
All inputs are finite; a program needn't handle non-finite values. No bound on the sum of `loss_mask` on one device may be relied on, other than what follows from the above.
Results may differ from a plain program's by a relative error of at most 0.035.
Values may be sent and summed in bfloat16 or wider, within the bound.
A program may use at most 32 MiB of HBM per device.

v0:
```python
import jax
import jax.numpy as jnp
from jax import lax
from jax.sharding import Mesh
from jax.sharding import PartitionSpec as P

D = 8192
SEQ = 40
IMG = 16
COL = ("col_0", "col_1")


dpo_beta = 0.1
norm_eps = 1e-06


def from_everyone(array, axis):
    peers = lax.axis_size(axis)
    return lax.all_to_all(
        jnp.broadcast_to(array[None], (peers, *array.shape)), axis, 0, 0, tiled=True
    )


def joined_along(blocks, dim):
    lengths = list(blocks.shape[1:])
    lengths[dim] *= blocks.shape[0]
    return jnp.moveaxis(blocks, 0, dim).reshape(lengths)


def collect(array, axis, dim):
    blocks = from_everyone(array, axis)
    return joined_along(blocks, dim)


def split_up(array, dim, peers):
    lengths = array.shape
    blocks = array.reshape(*lengths[:dim], peers, lengths[dim] // peers, *lengths[dim + 1 :])
    return jnp.moveaxis(blocks, dim, 0)


def sum_at_owner(array, axis, dim):
    blocks = split_up(array, dim, lax.axis_size(axis))
    arrived = lax.all_to_all(blocks, axis, split_axis=0, concat_axis=0, tiled=True)
    return arrived.astype(jnp.float32).sum(axis=0)


def over_copies(array, axis):
    return from_everyone(array, axis).sum(axis=0)


def together(arrays, axis):
    ravelled, at, gathered = (jnp.concatenate([a.reshape(-1) for a in arrays]), 0, [])
    subtotal = over_copies(ravelled, axis)
    for a in arrays:
        gathered.append(subtotal[at : at + a.size].reshape(a.shape))
        at += a.size
    return tuple(gathered)


def stacked_from(array, axes, turns):
    blocks = array
    for k in turns:
        blocks = lax.all_gather(blocks, axes[k])
    done = turns[::-1]
    back = [done.index(k) for k in range(len(axes))]
    blocks = blocks.transpose(*back, *range(len(axes), blocks.ndim))
    return blocks.reshape(-1, *array.shape)


def gathered_by_axis(array, axes, turns, dim):
    return joined_along(stacked_from(array, axes, turns), dim)


def place_images(text_rows, images, offsets):
    tokens = text_rows.shape[0]
    global_pos = jnp.arange(tokens, dtype=jnp.int32)
    position = global_pos % SEQ
    seq_id = global_pos // SEQ
    first_img = offsets[seq_id]
    inside = (position >= first_img) & (position < first_img + IMG)
    source = jnp.clip(seq_id * IMG + position - first_img, 0, images.shape[0] - 1)
    return jnp.where(inside[:, None], jnp.take(images, source, axis=0), text_rows)


def dpo_terms(totals):
    policy = totals[0]
    frozen = totals[1]
    margin = policy[0::2] - frozen[0::2] - (policy[1::2] - frozen[1::2])
    loss_value = jnp.mean(jax.nn.softplus(-dpo_beta * margin))
    dmargin = -dpo_beta * jax.nn.sigmoid(-dpo_beta * margin) / margin.shape[0]
    return (loss_value, dmargin)


def dot_transposed(left, right):
    return lax.dot_general(
        left, right, (((1,), (1,)), ((), ())), preferred_element_type=jnp.float32
    )


def local(
    text_embeds,
    image_embeds,
    offsets,
    lengths,
    loss_mask,
    norm_gain,
    unembed_rows,
    gate_up,
    down_proj,
):
    text_full = collect(text_embeds, "row", 0)
    images = collect(image_embeds, ("mp", "row"), 0)
    inputs = place_images(text_full, images, offsets)
    tokens = inputs.shape[0]
    local_rows = tokens // lax.axis_size("row")
    hidden_width = gate_up.shape[3]
    weight = gate_up[0].reshape(gate_up.shape[1], 2 * hidden_width)
    down_block = down_proj[0]
    row_start = lax.axis_index("row") * local_rows
    pre_sums = sum_at_owner(
        jnp.dot(inputs, weight, preferred_element_type=jnp.float32).astype(jnp.bfloat16), COL, 0
    )
    gate_part = pre_sums[:, :hidden_width]
    up_part = pre_sums[:, hidden_width:]
    hidden = (jax.nn.silu(gate_part) * up_part).astype(jnp.bfloat16)
    out_partial = jnp.dot(collect(hidden, COL, 0), down_block, preferred_element_type=jnp.float32)
    block_out = sum_at_owner(out_partial.astype(jnp.bfloat16), "row", 0)
    own_rows = lax.dynamic_slice_in_dim(inputs, row_start, local_rows, 0)
    residual = own_rows.astype(jnp.float32) + block_out
    coeff = norm_gain[0].astype(jnp.float32)[None, :] * unembed_rows[0].astype(jnp.float32)
    squares, cross_term = together(
        (jnp.sum(residual * residual, axis=1), jnp.sum(residual * coeff, axis=1)), COL
    )
    inv_rms = lax.rsqrt(squares / D + norm_eps)
    tok_score = cross_term * inv_rms
    global_pos = row_start + jnp.arange(local_rows, dtype=jnp.int32)
    position = global_pos % SEQ
    seq_id = global_pos // SEQ
    scored = ((position < lengths[seq_id]) & (loss_mask == 1)).astype(jnp.float32)
    seq_count = offsets.shape[0]
    onehot = (seq_id[:, None] == jnp.arange(seq_count, dtype=jnp.int32)[None, :]).astype(
        jnp.float32
    )
    seq_part = jnp.dot(scored * tok_score, onehot, precision=lax.Precision.HIGHEST)
    model_id = lax.axis_index("mp")
    score_slots = (jnp.arange(2, dtype=jnp.int32) == model_id).astype(jnp.float32)[
        :, None
    ] * seq_part[None, :]
    totals = over_copies(score_slots, ("mp", "row"))
    loss_value, dmargin = dpo_terms(totals)
    policy_flag = (model_id == 0).astype(jnp.float32)
    seq_grad = policy_flag * jnp.stack([dmargin, -dmargin], axis=1).reshape(seq_count)
    dscore = scored * jnp.dot(onehot, seq_grad, precision=lax.Precision.HIGHEST)
    dresid = dscore[:, None] * (
        inv_rms[:, None] * coeff - (cross_term * inv_rms**3 / D)[:, None] * residual
    )
    dy_full = collect(dresid.astype(jnp.bfloat16), "row", 0)
    dhidden = sum_at_owner(dot_transposed(dy_full, down_block).astype(jnp.bfloat16), COL, 0)
    sigmoid_gate = jax.nn.sigmoid(gate_part)
    gate_grad = dhidden * up_part * sigmoid_gate * (1.0 + gate_part * (1.0 - sigmoid_gate))
    up_grad = dhidden * gate_part * sigmoid_gate
    pre_grad = jnp.concatenate([gate_grad, up_grad], axis=1).astype(jnp.bfloat16)
    input_partial = dot_transposed(gathered_by_axis(pre_grad, COL, (0, 1), 0), weight)
    placed = lax.dynamic_update_slice_in_dim(jnp.zeros_like(input_partial), dresid, row_start, 0)
    input_grad = sum_at_owner((input_partial + placed).astype(jnp.bfloat16), ("mp", "row"), 0)
    return (loss_value, input_grad)


def solution(mesh):
    split = Mesh(
        mesh.devices.reshape(mesh.shape["mp"], mesh.shape["row"], 16, 2),
        ("mp", "row", "col_0", "col_1"),
    )
    in_specs = (
        P("row", COL),
        P(("mp", "row"), COL),
        P(),
        P(),
        P("row"),
        P("mp", COL),
        P("mp", "row", COL),
        P("mp", COL, None, "row"),
        P("mp", "row", COL),
    )
    out_specs = (P(), P(("mp", "row"), COL))
    return jax.shard_map(local, mesh=split, in_specs=in_specs, out_specs=out_specs, check_vma=False)
```

profile of v0, /device:TPU:1, one launch (start us, length us, event | category | flops | bytes accessed | tf_op | source)
XLA Modules:
  0.0 422.8 jit_solution(8430935883207078191)
XLA Ops:
  7.2 1.4 broadcast_in_dim.38
  8.6 10.5 %all-to-all-start = ((bf16[32,2,256]{2,1,0:T(2,128)(2,1)}), bf16[32,2,256]{2,1,0:T(2,128)(2,1)S(1)}, u32[]{:S(2)}, u32[]{:S(2)}) async-start(bf16[32,2,256]{2,1,0:T(2,128)(2,1)} %broadcast_in_dim.38), calls=%async_computation | async-start | bytes 65536 | tf_op jit(solution)/shard_map/all_to_all | solution.py:19
  19.1 1.5 fusion.40
  20.6 0.5 broadcast.461
  21.1 3.3 fusion.39
  24.4 0.1 gather.20
  24.5 3.3 all-to-all-done
  27.8 1.4 broadcast_in_dim.40
  29.1 5.7 %all-to-all-start.1 = ((bf16[16,10,256]{2,1,0:T(8,128)(2,1)}), bf16[16,10,256]{2,1,0:T(8,128)(2,1)S(1)}, u32[]{:S(2)}, u32[]{:S(2)}) async-start(bf16[16,10,256]{2,1,0:T(8,128)(2,1)} %broadcast_in_dim.40), calls=%async_computation.1 | async-start | bytes 262144 | tf_op jit(solution)/shard_map/all_to_all | solution.py:19
  34.8 0.9 gather_fusion.1
  35.8 8.2 %all-to-all-done.1 = bf16[16,10,256]{2,1,0:T(8,128)(2,1)S(1)} async-done(((bf16[16,10,256]{2,1,0:T(8,128)(2,1)}), bf16[16,10,256]{2,1,0:T(8,128)(2,1)S(1)}, u32[]{:S(2)}, u32[]{:S(2)}) %all-to-all-start.1) | async-done | bytes 81952 | tf_op jit(solution)/shard_map/all_to_all | solution.py:19
  44.0 0.1 select_select_fusion
  44.2 0.5 copy-done.3
  44.7 0.8 convolution_convert_fusion
  45.5 1.6 reshape.266
  47.0 114.1 %all_to_all.51 = bf16[32,5,3696]{2,1,0:T(8,128)(2,1)S(1)} all-to-all(bf16[32,5,3696]{2,1,0:T(8,128)(2,1)} %reshape.266), channel_id=1, replica_groups=mesh['mp'=2,'row'=16,'col_0'=16,'col_1'=2] {'col_0','col_1'}, dimensions={0} | all-to-all | bytes 2365440 | tf_op jit(solution)/shard_map/all_to_all | solution.py:43
  161.1 0.4 convert_reduce_fusion
  161.5 0.6 copy-done.4
  162.2 0.1 multiply_convert_fusion.2
  162.2 1.0 broadcast_in_dim.44
  163.3 4.1 all-to-all-start.3
  167.4 0.7 gather_fusion
  168.1 52.3 %all-to-all-done.3 = bf16[32,5,1848]{2,1,0:T(8,128)(2,1)S(1)} async-done(((bf16[32,5,1848]{2,1,0:T(8,128)(2,1)}), bf16[32,5,1848]{2,1,0:T(8,128)(2,1)S(1)}, u32[]{:S(2)}, u32[]{:S(2)}) %all-to-all-start.3) | async-done | bytes 591392 | tf_op jit(solution)/shard_map/all_to_all | solution.py:19
  220.4 0.4 reshape.267
  220.9 2.3 convolution_convert_fusion.2
  223.1 1.6 reshape.268
  224.7 3.5 all-to-all-start.4
  228.4 0.9 reshape.265
  229.4 8.4 %all-to-all-done.4 = bf16[16,10,256]{2,1,0:T(8,128)(2,1)S(1)} async-done(((bf16[16,10,256]{2,1,0:T(8,128)(2,1)}), bf16[16,10,256]{2,1,0:T(8,128)(2,1)S(1)}, u32[]{:S(2)}, u32[]{:S(2)}) %all-to-all-start.4) | async-done | bytes 81952 | tf_op jit(solution)/shard_map/all_to_all | solution.py:43
  237.8 0.9 multiply_reduce_fusion
  238.8 0.6 broadcast_in_dim.45
  239.4 5.3 %all-to-all-start.5 = ((f32[32,1,20]{2,1,0:T(1,128)}), f32[32,1,20]{2,1,0:T(1,128)S(1)}, u32[]{:S(2)}, u32[]{:S(2)}) async-start(f32[32,1,20]{2,1,0:T(1,128)} %broadcast_in_dim.45), calls=%async_computation.5 | async-start | bytes 32768 | tf_op jit(solution)/shard_map/all_to_all | solution.py:19
  244.7 11.9 %all-to-all-done.5 = f32[32,1,20]{2,1,0:T(1,128)S(1)} async-done(((f32[32,1,20]{2,1,0:T(1,128)}), f32[32,1,20]{2,1,0:T(1,128)S(1)}, u32[]{:S(2)}, u32[]{:S(2)}) %all-to-all-start.5) | async-done | bytes 2592 | tf_op jit(solution)/shard_map/all_to_all | solution.py:19
  256.6 0.2 convolution_bitcast_fusion.1
  256.9 0.6 broadcast_in_dim.46
  257.5 3.9 all-to-all-start.6
  261.5 8.5 %all-to-all-done.6 = f32[32,2,4]{2,1,0:T(2,128)S(1)} async-done(((f32[32,2,4]{2,1,0:T(2,128)}), f32[32,2,4]{2,1,0:T(2,128)S(1)}, u32[]{:S(2)}, u32[]{:S(2)}) %all-to-all-start.6) | async-done | bytes 1056 | tf_op jit(solution)/shard_map/all_to_all | solution.py:19
  270.0 0.1 slice.39
  270.1 0.1 slice.37
  270.2 0.1 slice.38
  270.3 0.1 slice.35
  270.4 0.1 copy.32
  270.5 0.1 reshape.321
  270.6 0.2 fusion
  270.9 12.0 %all_to_all.52 = bf16[16,10,256]{2,1,0:T(8,128)(2,1)S(1)} all-to-all(bf16[16,10,256]{2,1,0:T(8,128)(2,1)S(1)} %broadcast_in_dim.47), channel_id=1, replica_groups=mesh['mp'=2,'row'=16,'col_0'=16,'col_1'=2] {'row'}, dimensions={0} | all-to-all | bytes 163840 | tf_op jit(solution)/shard_map/all_to_all | solution.py:19
  282.9 0.7 reshape.269
  283.6 1.4 convolution_convert_fusion.1
  285.0 0.3 reshape.270
  285.3 59.1 %all_to_all.53 = bf16[32,5,1848]{2,1,0:T(8,128)(2,1)S(1)} all-to-all(bf16[32,5,1848]{2,1,0:T(8,128)(2,1)S(1)} %reshape.270), channel_id=1, replica_groups=mesh['mp'=2,'row'=16,'col_0'=16,'col_1'=2] {'col_0','col_1'}, dimensions={0} | all-to-all | bytes 1182720 | tf_op jit(solution)/shard_map/all_to_all | solution.py:43
  344.4 0.2 convert_reduce_fusion.1
  344.6 0.1 fusion.4
  344.7 0.1 pad_maximum_fusion
  344.8 25.1 %all_gather.10 = bf16[16,5,3696]{2,1,0:T(8,128)(2,1)S(1)} all-gather(bf16[1,5,3696]{2,1,0:T(8,128)(2,1)S(1)} %pad_maximum_fusion), channel_id=1, replica_groups=mesh['mp'=2,'row'=16,'col_0'=16,'col_1'=2] {'col_0'}, dimensions={0}, use_global_device_ids=true | all-gather | bytes 628320 | tf_op jit(solution)/shard_map/all_gather | solution.py:63
  369.9 0.9 copy.33
  370.8 20.5 %all-gather.3.cloned.1.call-done = bf16[32,5,3696]{2,0,1:T(8,128)(2,1)} async-done(((bf16[16,5,3696]{2,0,1:T(8,128)(2,1)}), bf16[32,5,3696]{2,0,1:T(8,128)(2,1)}) %all-gather.3.cloned.1.call-update) | async-done | bytes 1182736 | tf_op jit(solution)/shard_map/all_gather | solution.py:63
  391.2 3.0 copy.34
  394.2 2.1 reshape_reshape.3
  396.3 0.5 fusion.41
  396.9 0.2 add.222
  397.1 0.7 reshape.271
  397.8 6.8 %all-to-all-start.9 = ((bf16[32,5,256]{2,1,0:T(8,128)(2,1)}), bf16[32,5,256]{2,1,0:T(8,128)(2,1)S(1)}, u32[]{:S(2)}, u32[]{:S(2)}) async-start(bf16[32,5,256]{2,1,0:T(8,128)(2,1)} %reshape.271), calls=%async_computation.9 | async-start | bytes 262144 | tf_op jit(solution)/shard_map/all_to_all | solution.py:43
  404.6 0.6 fusion.31
  405.9 8.3 %all-to-all-done.9 = bf16[32,5,256]{2,1,0:T(8,128)(2,1)S(1)} async-done(((bf16[32,5,256]{2,1,0:T(8,128)(2,1)}), bf16[32,5,256]{2,1,0:T(8,128)(2,1)S(1)}, u32[]{:S(2)}, u32[]{:S(2)}) %all-to-all-start.9) | async-done | bytes 81952 | tf_op jit(solution)/shard_map/all_to_all | solution.py:43
  414.2 0.6 convert_reduce_fusion.2
  (48 shorter events, 1.1 us)
Async XLA Ops:
  7.2 37.5 %copy-start = (bf16[1,256,2,1848]{1,3,2,0:T(8,128)(2,1)S(1)}, bf16[1,256,2,1848]{1,3,2,0:T(8,128)(2,1)}, u32[]{:S(2)}) copy-start(bf16[1,256,2,1848]{1,3,2,0:T(8,128)(2,1)} %param.16) | copy-start | bytes 5677060
  8.6 19.1 %all-to-all-start = ((bf16[32,2,256]{2,1,0:T(2,128)(2,1)}), bf16[32,2,256]{2,1,0:T(2,128)(2,1)S(1)}, u32[]{:S(2)}, u32[]{:S(2)}) async-start(bf16[32,2,256]{2,1,0:T(2,128)(2,1)} %broadcast_in_dim.38), calls=%async_computation | async-start | bytes 65536 | tf_op jit(solution)/shard_map/all_to_all | solution.py:19
  29.1 14.9 %all-to-all-start.1 = ((bf16[16,10,256]{2,1,0:T(8,128)(2,1)}), bf16[16,10,256]{2,1,0:T(8,128)(2,1)S(1)}, u32[]{:S(2)}, u32[]{:S(2)}) async-start(bf16[16,10,256]{2,1,0:T(8,128)(2,1)} %broadcast_in_dim.40), calls=%async_computation.1 | async-start | bytes 262144 | tf_op jit(solution)/shard_map/all_to_all | solution.py:19
  35.8 8.3 %copy-start.6 = (bf16[160,256]{1,0:T(8,128)(2,1)}, bf16[160,256]{1,0:T(8,128)(2,1)S(1)}, u32[]{:S(2)}) copy-start(bf16[160,256]{1,0:T(8,128)(2,1)S(1)} %gather_fusion.1) | copy-start | bytes 245764
  44.0 0.6 copy-start.3
  161.5 0.6 copy-start.4
  162.2 5.2 %copy-start.1 = (s32[4]{0:T(128)S(1)}, s32[4]{0:T(128)}, u32[]{:S(2)}) copy-start(s32[4]{0:T(128)} %param.12) | copy-start | bytes 52
  163.3 57.1 %all-to-all-start.3 = ((bf16[32,5,1848]{2,1,0:T(8,128)(2,1)}), bf16[32,5,1848]{2,1,0:T(8,128)(2,1)S(1)}, u32[]{:S(2)}, u32[]{:S(2)}) async-start(bf16[32,5,1848]{2,1,0:T(8,128)(2,1)} %broadcast_in_dim.44), calls=%async_computation.3 | async-start | bytes 1966080 | tf_op jit(solution)/shard_map/all_to_all | solution.py:19
  168.1 60.1 %copy-start.9 = (s32[10]{0:T(128)S(1)}, s32[10]{0:T(128)}, u32[]{:S(2)}) copy-start(s32[10]{0:T(128)} %param.13) | copy-start | bytes 124
  168.1 60.2 %copy-start.8 = (bf16[1,256]{1,0:T(2,128)(2,1)S(1)}, bf16[1,256]{1,0:T(2,128)(2,1)}, u32[]{:S(2)}) copy-start(bf16[1,256]{1,0:T(2,128)(2,1)} %param.14) | copy-start | bytes 1540
  168.1 69.7 %copy-start.7 = (bf16[1,10,256]{2,1,0:T(8,128)(2,1)S(1)}, bf16[1,10,256]{2,1,0:T(8,128)(2,1)}, u32[]{:S(2)}) copy-start(bf16[1,10,256]{2,1,0:T(8,128)(2,1)} %param.15) | copy-start | bytes 15364
  220.8 62.8 %copy-start.2 = (bf16[1,1848,256]{2,1,0:T(8,128)(2,1)S(1)}, bf16[1,1848,256]{2,1,0:T(8,128)(2,1)}, u32[]{:S(2)}) copy-start(bf16[1,1848,256]{2,1,0:T(8,128)(2,1)} %param.17) | copy-start | bytes 2838532
  224.7 13.1 %all-to-all-start.4 = ((bf16[16,10,256]{2,1,0:T(8,128)(2,1)}), bf16[16,10,256]{2,1,0:T(8,128)(2,1)S(1)}, u32[]{:S(2)}, u32[]{:S(2)}) async-start(bf16[16,10,256]{2,1,0:T(8,128)(2,1)} %reshape.268), calls=%async_computation.4 | async-start | bytes 262144 | tf_op jit(solution)/shard_map/all_to_all | solution.py:43
  239.4 17.2 %all-to-all-start.5 = ((f32[32,1,20]{2,1,0:T(1,128)}), f32[32,1,20]{2,1,0:T(1,128)S(1)}, u32[]{:S(2)}, u32[]{:S(2)}) async-start(f32[32,1,20]{2,1,0:T(1,128)} %broadcast_in_dim.45), calls=%async_computation.5 | async-start | bytes 32768 | tf_op jit(solution)/shard_map/all_to_all | solution.py:19
  257.5 12.5 %all-to-all-start.6 = ((f32[32,2,4]{2,1,0:T(2,128)}), f32[32,2,4]{2,1,0:T(2,128)S(1)}, u32[]{:S(2)}, u32[]{:S(2)}) async-start(f32[32,2,4]{2,1,0:T(2,128)} %broadcast_in_dim.46), calls=%async_computation.6 | async-start | bytes 65536 | tf_op jit(solution)/shard_map/all_to_all | solution.py:19
  261.4 129.9 %all-gather.3.cloned.1.call-start = ((), (), s32[]{:S(2)}) async-start(), calls=%async_computation.10 | async-start | bytes 1781760 | tf_op jit(solution)/shard_map/all_gather | solution.py:63
  285.2 59.3 %copy-start.5 = (f32[5,3696]{1,0:T(8,128)S(1)}, f32[5,3696]{1,0:T(8,128)}, u32[]{:S(2)}) copy-start(f32[5,3696]{1,0:T(8,128)} %copy-done.4) | copy-start | bytes 221764
  397.8 16.4 %all-to-all-start.9 = ((bf16[32,5,256]{2,1,0:T(8,128)(2,1)}), bf16[32,5,256]{2,1,0:T(8,128)(2,1)S(1)}, u32[]{:S(2)}, u32[]{:S(2)}) async-start(bf16[32,5,256]{2,1,0:T(8,128)(2,1)} %reshape.271), calls=%async_computation.9 | async-start | bytes 262144 | tf_op jit(solution)/shard_map/all_to_all | solution.py:43
Sparse Core Ops, SparseCore 0:
  370.9 20.3 all-gather.2
where the time goes:
time: 424 us; the launch traced here: 423 us
  blocking collectives  210 us (50%)
  waiting for transfers between devices  121 us (29%)
  starting transfers between devices  39.7 us (9%)
  local copies, waits for them, and re-layouts  22.9 us (5%)
  between operations  16.2 us (4%)
  other arithmetic  7.08 us (2%)
  matrix products  5.32 us (1%)
    all_to_all x2, blocking collectives, sum_at_owner(): lax.all_to_all(blocks, axis, split_axis=0, concat_axis=0, tiled=True)  173 us
    all_to_all x5, waiting for transfers between devices, from_everyone(): lax.all_to_all(jnp.broadcast_to(array[None], (peers, *array.shape)), axis...  84.1 us
    all_to_all x5, starting transfers between devices, from_everyone(): lax.all_to_all(jnp.broadcast_to(array[None], (peers, *array.shape)), axis...  29.4 us
    all_gather x1, blocking collectives, stacked_from(): blocks = lax.all_gather(blocks, axes[k])  25.1 us
    all_gather x1, waiting for transfers between devices, stacked_from(): blocks = lax.all_gather(blocks, axes[k])  20.5 us
    all_to_all x2, waiting for transfers between devices, sum_at_owner(): lax.all_to_all(blocks, axis, split_axis=0, concat_axis=0, tiled=True)  16.7 us
    all_to_all x1, blocking collectives, from_everyone(): lax.all_to_all(jnp.broadcast_to(array[None], (peers, *array.shape)), axis...  12 us
    all_to_all x2, starting transfers between devices, sum_at_owner(): lax.all_to_all(blocks, axis, split_axis=0, concat_axis=0, tiled=True)  10.3 us
  transfers between devices with their start and end apart: 8, of which 8 were waited for; matrix products, arithmetic and copies ran while one was open for 2% of the time, Pallas kernels for 0%

commit v1 on v0

v1 whole, which is shorter than its diff:
```python
import jax
import jax.numpy as jnp
from jax import lax
from jax.experimental import pallas as pl
from jax.experimental.pallas import tpu as pltpu
from jax.sharding import PartitionSpec as P

D = 8192
SEQ = 40
IMG = 16
ROWS = 16
CHIPS = 16
OWN = 10
HALF = 80
TILE = 128
TILES = 15
LAST = 56
BETA = 0.1
EPS = 1e-06
MESH = pl.DeviceIdType.MESH
LEADERS = (0, 3, -3, 6, -6)
F32 = jnp.float32
BF16 = jnp.bfloat16


def iota(shape, dim):
    return lax.broadcasted_iota(jnp.int32, shape, dim)


def dot(a, b, precision=None):
    return jnp.dot(a, b, preferred_element_type=F32, precision=precision)


def dot_t(a, b):
    return lax.dot_general(a, b, (((1,), (1,)), ((), ())), preferred_element_type=F32)


def kernel(
    text_ref,
    image_ref,
    offsets_ref,
    lengths_ref,
    mask_ref,
    gain_ref,
    unembed_ref,
    gate_up_ref,
    down_ref,
    loss_ref,
    grad_ref,
    w_s,
    d_s,
    tail_s,
    in_buf,
    un_buf,
    x_s,
    p_s,
    px_s,
    l1_s,
    lx_s,
    s_s,
    l2_s,
    h_s,
    q_s,
    qx_s,
    m1_s,
    mx_s,
    t_s,
    m2_s,
    g_s,
    gate_s,
    up_s,
    so_s,
    ro_s,
    res_buf,
    res_s,
    sum_buf,
    row_buf,
    sf_s,
    rf_s,
    w_sem,
    in_sem,
    un_sem,
    fx_sem,
    f1_sem,
    f2_sem,
    hz_sem,
    hc_sem,
    bx_sem,
    b1_sem,
    b2_sem,
    gz_sem,
    gc_sem,
    ro_sem,
    res_sem,
    sum_sem,
    row_sem,
    rf_sem,
):
    mp = lax.axis_index("mp")
    row = lax.axis_index("row")
    col = lax.axis_index("col")
    plane = mp * ROWS + row
    z = lax.div(col, 2)
    core = lax.rem(col, 2)

    def chip(offset):
        return lax.rem(z + offset + 2 * CHIPS, CHIPS)

    def at_chip(where):
        return {"col": 2 * where + core}

    def plane_id(index):
        return {"mp": lax.div(index, ROWS), "row": lax.rem(index, ROWS)}

    partner = {"col": 2 * z + 1 - core}

    def remote(src, dst, sems, index, device):
        return pltpu.make_async_remote_copy(
            src_ref=src,
            dst_ref=dst,
            send_sem=sems.at[0, index],
            recv_sem=sems.at[1, index],
            device_id=device,
            device_id_type=MESH,
        )

    def wait_bytes(ref, sem):
        pltpu.make_async_copy(ref, ref, sem).wait()

    w_copy = pltpu.make_async_copy(gate_up_ref, w_s, w_sem.at[0])
    d_copy = pltpu.make_async_copy(down_ref, d_s, w_sem.at[1])
    w_copy.start()
    d_copy.start()

    barrier = pltpu.get_barrier_semaphore()

    def greet_plane(d, carry):
        other = lax.rem(plane + d, 2 * ROWS)
        pl.semaphore_signal(barrier, inc=1, device_id=plane_id(other), device_id_type=MESH)
        return carry

    def greet_col(d, carry):
        other = lax.rem(col + d, 2 * CHIPS)
        pl.semaphore_signal(barrier, inc=1, device_id={"col": other}, device_id_type=MESH)
        return carry

    lax.fori_loop(1, 2 * ROWS, greet_plane, 0)
    lax.fori_loop(1, 2 * CHIPS, greet_col, 0)

    stage = jnp.concatenate(
        [
            text_ref[...].astype(F32),
            image_ref[...].astype(F32),
            jnp.zeros((4, text_ref.shape[1]), F32),
        ],
        axis=0,
    )
    in_buf[plane] = stage.astype(BF16)
    own_unembed = jnp.concatenate(
        [unembed_ref[...].astype(F32), jnp.zeros((6, text_ref.shape[1]), F32)], axis=0
    )
    un_buf[row] = own_unembed.astype(BF16)
    gain = gain_ref[...].astype(F32)
    pl.semaphore_wait(barrier, 2 * (2 * ROWS - 1))

    def to_plane(make):
        def send(d, carry):
            make(lax.rem(plane + d, 2 * ROWS)).start()
            return carry

        lax.fori_loop(1, 2 * ROWS, send, 0)

    def to_row(make):
        def send(d, carry):
            make(lax.rem(row + d, ROWS)).start()
            return carry

        lax.fori_loop(1, ROWS, send, 0)

    to_plane(lambda o: remote(in_buf.at[plane], in_buf.at[plane], in_sem, 0, plane_id(o)))
    to_row(lambda o: remote(un_buf.at[row], un_buf.at[row], un_sem, 0, {"row": o}))

    token = iota((SEQ * 4, 2 * ROWS * 16), 0)
    source = iota((SEQ * 4, 2 * ROWS * 16), 1)
    position = lax.rem(token, SEQ)
    seq_id = lax.div(token, SEQ)
    first = jnp.where(
        seq_id == 0,
        offsets_ref[0],
        jnp.where(seq_id == 1, offsets_ref[1], jnp.where(seq_id == 2, offsets_ref[2], offsets_ref[3])),
    )
    inside = (position >= first) & (position < first + IMG)
    image_row = seq_id * IMG + position - first
    from_image = lax.shift_right_arithmetic(image_row, 1) * 16 + OWN + (image_row & 1)
    from_text = (mp * ROWS + lax.div(token, OWN)) * 16 + lax.rem(token, OWN)
    pick = (source == jnp.where(inside, from_image, from_text)).astype(BF16)

    w_copy.wait()
    d_copy.wait()
    tail_s[...] = jnp.zeros_like(tail_s)
    start = (TILES - 1) * TILE
    tail_s[0, :LAST] = w_s[0, start:]
    tail_s[1, :LAST] = w_s[1, start:]
    tail_s[2, :LAST] = d_s[start:]

    def weight(j):
        if j == TILES - 1:
            return jnp.concatenate([tail_s[0], tail_s[1]], axis=0)
        rows = slice(j * TILE, (j + 1) * TILE)
        return jnp.concatenate([w_s[0, rows], w_s[1, rows]], axis=0)

    def down(j):
        return tail_s[2] if j == TILES - 1 else d_s[j * TILE : (j + 1) * TILE]

    wait_bytes(in_buf.at[pl.ds(0, 2 * ROWS - 1)], in_sem.at[1, 0])
    gathered = in_buf[...].reshape(2 * ROWS * 16, text_ref.shape[1])
    x_s[...] = dot(pick, gathered).astype(BF16)

    def reduce_start(partial, p, px, sx):
        for j in range(TILES):
            p[j] = partial(j).astype(BF16).reshape(2, HALF, p.shape[3])
            remote(p.at[j, 1 - core], px.at[j], sx, j, partner).start()

    def level_one():
        out = []
        for k, lead in enumerate(LEADERS):
            for side, o in enumerate((lead - 1, lead + 1)):
                out.append((o, lead, 2 * k + side))
        return sorted(out, key=lambda e: -abs(e[1]))

    def reduce_end(p, px, l1, lx, s, l2, sx, s1, s2):
        def pair(j):
            remote(p.at[j, 1 - core], px.at[j], sx, j, partner).wait_recv()
            return p[j, core].astype(F32) + px[j].astype(F32)

        def first_sum(o):
            j = chip(-o)

            def do(send):
                @pl.when(j != TILES)
                def _():
                    p[j, core] = pair(j).astype(BF16)
                    send(j)

            return do

        far = 2 - 4 * core
        first_sum(8)(lambda j: remote(p.at[j, core], lx, s1, 10, at_chip(chip(-far))).start())
        for o, lead, slot in level_one():
            first_sum(o)(
                lambda j, o=o, lead=lead, slot=slot: remote(
                    p.at[j, core], l1.at[slot], s1, slot, at_chip(chip(lead - o))
                ).start()
            )
        for k in (3, 4, 1, 2):
            lead = LEADERS[k]
            j = chip(-lead)

            @pl.when(j != TILES)
            def _(k=k, lead=lead, j=j):
                total = pair(j)
                for slot in (2 * k, 2 * k + 1):
                    remote(l1.at[slot], l1.at[slot], s1, slot, partner).wait_recv()
                    total = total + l1[slot].astype(F32)
                if abs(lead) == 6:
                    extra = core == (0 if lead == 6 else 1)

                    @pl.when(extra)
                    def _():
                        remote(lx, lx, s1, 10, partner).wait_recv()
                        s[k - 1] = (total + lx[...].astype(F32)).astype(BF16)

                    @pl.when(jnp.logical_not(extra))
                    def _():
                        s[k - 1] = total.astype(BF16)
                else:
                    s[k - 1] = total.astype(BF16)
                remote(s.at[k - 1], l2.at[k - 1], s2, k - 1, at_chip(j)).start()

    def reduce_final(p, px, l1, l2, sx, s1, s2):
        remote(p.at[z, 1 - core], px.at[z], sx, z, partner).wait_recv()
        total = p[z, core].astype(F32) + px[z].astype(F32)
        for slot in (0, 1):
            remote(l1.at[slot], l1.at[slot], s1, slot, partner).wait_recv()
            total = total + l1[slot].astype(F32)
        for k in range(4):
            remote(s_any(l2, k), s_any(l2, k), s2, k, partner).wait_recv()
            total = total + l2[k].astype(F32)
        return total

    def s_any(ref, k):
        return ref.at[k]

    def reduce_sent(p, px, l1, lx, s, l2, sx, s1, s2):
        for j in range(TILES):
            remote(p.at[j, 1 - core], px.at[j], sx, j, partner).wait_send()
        for o, slot in [(8, 10)] + [(o, slot) for o, _, slot in level_one()]:

            @pl.when(chip(-o) != TILES)
            def _(slot=slot):
                remote(lx, lx, s1, slot, partner).wait_send()

        for k in range(1, 5):

            @pl.when(chip(-LEADERS[k]) != TILES)
            def _(k=k):
                remote(lx, lx, s2, k - 1, partner).wait_send()

    def gather_all(g, sz, sc):
        sends = []

        def send(block, by, o, when):
            n = len(sends)
            pltpu.make_async_remote_copy(
                src_ref=g.at[block, core],
                dst_ref=g.at[block, core],
                send_sem=sz.at[0, n],
                recv_sem=sz.at[1, o + 7],
                device_id=at_chip(chip(by)),
                device_id_type=MESH,
            ).start()
            sends.append((n, when))

        def across(block):
            remote(g.at[block, core], g.at[block, core], sc, block, partner).start()

        mine = z != TILES

        @pl.when(mine)
        def _():
            for o in (6, -6, 3, -3, 1, -1):
                send(z, o, o, mine)
            across(z)

        for o in (1, -1, 3, -3, 6, -6, 2, -2, 4, -4, 5, -5, 7, -7, 8):
            block = chip(-o)
            there = block != TILES
            relays = core == (0 if o == 6 else 1)
            both = there & relays

            @pl.when(there)
            def _(o=o, block=block, there=there, relays=relays, both=both):
                pltpu.make_async_remote_copy(
                    src_ref=g.at[block, core],
                    dst_ref=g.at[block, core],
                    send_sem=sz.at[0, 0],
                    recv_sem=sz.at[1, o + 7],
                    device_id=partner,
                    device_id_type=MESH,
                ).wait_recv()
                if o in (3, -3, 6, -6):
                    if abs(o) == 6:

                        @pl.when(relays)
                        def _():
                            send(block, 2 if o == 6 else -2, 8, both)

                    send(block, 1, o + 1, there)
                    send(block, -1, o - 1, there)
                across(block)

        for j in range(TILES):
            remote(g.at[j, core], g.at[j, core], sc, j, partner).wait()
        for n, when in sends:

            @pl.when(when)
            def _(n=n):
                remote(g.at[0, 0], g.at[0, 0], sz, n, partner).wait_send()

    x = x_s[...]
    reduce_start(lambda j: dot_t(x, weight(j)), p_s, px_s, fx_sem)
    forward = (p_s, px_s, l1_s, lx_s, s_s, l2_s, fx_sem, f1_sem, f2_sem)
    reduce_end(*forward)

    @pl.when(z != TILES)
    def _():
        pre = reduce_final(p_s, px_s, l1_s, l2_s, fx_sem, f1_sem, f2_sem)
        gate = pre[:, :TILE]
        up = pre[:, TILE:]
        gate_s[...] = gate
        up_s[...] = up
        h_s[z, core] = (gate * jax.nn.sigmoid(gate) * up).astype(BF16)

    gather_all(h_s, hz_sem, hc_sem)

    def hidden(j):
        return h_s[j].reshape(2 * HALF, TILE)

    out = dot(hidden(TILES - 1), down(TILES - 1))
    for j in range(0, TILES - 1, 2):
        both = jnp.concatenate([hidden(j), hidden(j + 1)], axis=1)
        out = out + dot(both, d_s[j * TILE : (j + 2) * TILE])

    slot_row = iota((ROWS * 16, SEQ * 4), 0)
    slot_token = iota((ROWS * 16, SEQ * 4), 1)
    spread = (
        (slot_token == lax.div(slot_row, 16) * OWN + lax.rem(slot_row, 16)) & (lax.rem(slot_row, 16) < OWN)
    ).astype(BF16)
    so_s[...] = dot(spread, out.astype(BF16)).astype(BF16).reshape(so_s.shape)
    to_row(lambda o: remote(so_s.at[o], ro_s.at[row], ro_sem, 0, {"row": o}))
    ro_s[row] = so_s[row]
    own_row = iota((16, SEQ * 4), 0)
    own_pick = ((iota((16, SEQ * 4), 1) == row * OWN + own_row) & (own_row < OWN)).astype(BF16)
    own_rows = dot(own_pick, x)
    coeff = own_unembed * gain
    wait_bytes(ro_s.at[pl.ds(0, ROWS - 1)], ro_sem.at[1, 0])
    residual = own_rows + jnp.sum(ro_s[...].astype(F32), axis=0)
    res_s[...] = residual

    square = (iota((16, 128), 0) == iota((16, 128), 1)).astype(F32)

    def as_row(values):
        return jnp.sum(values * square, axis=0, keepdims=True)

    def as_column(values):
        return jnp.sum(values * square, axis=1, keepdims=True)

    sums = jnp.concatenate(
        [
            as_row(jnp.sum(residual * residual, axis=1, keepdims=True)),
            as_row(jnp.sum(residual * coeff, axis=1, keepdims=True)),
        ],
        axis=0,
    )
    sum_buf[col] = sums

    def send_sums(d, carry):
        other = lax.rem(col + d, 2 * CHIPS)
        remote(sum_buf.at[col], sum_buf.at[col], sum_sem, 0, {"col": other}).start()
        return carry

    lax.fori_loop(1, 2 * CHIPS, send_sums, 0)
    res_buf[row] = residual.astype(BF16)

    @pl.when(mp == 0)
    def _():
        to_row(lambda o: remote(res_buf.at[row], res_buf.at[row], res_sem, 0, {"row": o}))

    lane = iota((1, 128), 1)
    masked = jnp.zeros((1, 128), jnp.int32)
    for t in range(OWN):
        masked = jnp.where(lane == t, mask_ref[t], masked)
    place = lax.rem(row, 4) * OWN + lane
    scored = ((place < lengths_ref[lax.div(row, 4)]) & (masked == 1) & (lane < OWN)).astype(F32)

    wait_bytes(sum_buf.at[pl.ds(0, 2 * CHIPS - 1)], sum_sem.at[1, 0])
    totals = jnp.sum(sum_buf[...], axis=0)
    squares = totals[0:1]
    cross = totals[1:2]
    inv_rms = lax.rsqrt(squares / D + EPS)
    by_coeff = scored * inv_rms
    by_residual = scored * (cross * inv_rms * inv_rms * inv_rms / D)
    row_buf[plane] = jnp.concatenate(
        [scored * (cross * inv_rms), by_coeff, by_residual, jnp.zeros((1, 128), F32)], axis=0
    )
    to_plane(lambda o: remote(row_buf.at[plane], row_buf.at[plane], row_sem, 0, plane_id(o)))
    wait_bytes(row_buf.at[pl.ds(0, 2 * ROWS - 1)], row_sem.at[1, 0])

    margins = []
    for q in range(2):
        acc = jnp.zeros((1, 128), F32)
        for r in range(8):
            policy = row_buf[8 * q + r][0:1]
            frozen = row_buf[ROWS + 8 * q + r][0:1]
            acc = acc + (policy - frozen if r < 4 else frozen - policy)
        margins.append(jnp.sum(acc, axis=1, keepdims=True))
    logits = [-BETA * m for m in margins]
    losses = [jnp.maximum(v, 0.0) + jnp.log1p(jnp.exp(-jnp.abs(v))) for v in logits]
    loss_ref[...] = (losses[0] + losses[1]) * 0.5
    dmargin = [-BETA * jax.nn.sigmoid(v) * 0.5 for v in logits]

    @pl.when(mp == 0)
    def _():
        wait_bytes(un_buf.at[pl.ds(0, ROWS - 1)], un_sem.at[1, 0])
        wait_bytes(res_buf.at[pl.ds(0, ROWS - 1)], res_sem.at[1, 0])
        rows = []
        for r in range(ROWS):
            grad = dmargin[r // 8] if (r // 4) % 2 == 0 else -dmargin[r // 8]
            terms = row_buf[r]
            rows.append(
                (
                    (as_column(terms[1:2]) * grad) * (un_buf[r].astype(F32) * gain)
                    - (as_column(terms[2:3]) * grad) * res_buf[r].astype(F32)
                ).astype(BF16)
            )
        spread_rows = jnp.concatenate(rows, axis=0)
        token_row = iota((SEQ * 4, ROWS * 16), 0)
        token_slot = iota((SEQ * 4, ROWS * 16), 1)
        compact = (token_slot == lax.div(token_row, OWN) * 16 + lax.rem(token_row, OWN)).astype(BF16)
        dy = dot(compact, spread_rows).astype(BF16)

        reduce_start(lambda j: dot_t(dy, down(j)), q_s, qx_s, bx_sem)
        backward = (q_s, qx_s, m1_s, mx_s, t_s, m2_s, bx_sem, b1_sem, b2_sem)
        reduce_end(*backward)

        @pl.when(z != TILES)
        def _():
            dhidden = reduce_final(q_s, qx_s, m1_s, m2_s, bx_sem, b1_sem, b2_sem)
            gate = gate_s[...]
            up = up_s[...]
            sig = jax.nn.sigmoid(gate)
            gate_grad = dhidden * up * sig * (1.0 + gate * (1.0 - sig))
            up_grad = dhidden * gate * sig
            g_s[z, core] = jnp.concatenate([gate_grad, up_grad], axis=1).astype(BF16)

        gather_all(g_s, gz_sem, gc_sem)
        total = jnp.zeros((SEQ * 4, text_ref.shape[1]), F32)
        for j in range(TILES):
            total = total + dot(g_s[j].reshape(2 * HALF, 2 * TILE), weight(j))
        first_pair = jnp.where(lax.div(row, 8) == 0, dmargin[0], dmargin[1])
        own_grad = jnp.where(lax.rem(lax.div(row, 4), 2) == 0, first_pair, -first_pair)
        own_coeff = own_unembed * gain
        dresidual = (as_column(by_coeff) * own_grad) * own_coeff - (
            as_column(by_residual) * own_grad
        ) * res_s[...]
        back_slot = iota((SEQ * 4, 16), 1)
        back = ((iota((SEQ * 4, 16), 0) == row * OWN + back_slot) & (back_slot < OWN)).astype(F32)
        total = total + dot(back, dresidual, lax.Precision.HIGHEST)
        out_row = iota((2 * ROWS * 8, SEQ * 4), 0)
        out_token = iota((2 * ROWS * 8, SEQ * 4), 1)
        by_owner = (
            (out_token == lax.div(out_row, 8) * 5 + lax.rem(out_row, 8)) & (lax.rem(out_row, 8) < 5)
        ).astype(F32)
        sf_s[...] = dot(by_owner, total, lax.Precision.HIGHEST).reshape(sf_s.shape)
        to_plane(lambda o: remote(sf_s.at[o], rf_s.at[row], rf_sem, 0, plane_id(o)))
        rf_s[row] = sf_s[row]
        wait_bytes(rf_s.at[pl.ds(0, ROWS - 1)], rf_sem.at[1, 0])
        reduce_sent(*backward)
        wait_bytes(res_buf.at[pl.ds(0, ROWS - 1)], res_sem.at[0, 0])
        wait_bytes(sf_s.at[pl.ds(0, 2 * ROWS - 1)], rf_sem.at[0, 0])

    @pl.when(mp == 1)
    def _():
        wait_bytes(un_buf.at[pl.ds(0, ROWS - 1)], un_sem.at[1, 0])
        wait_bytes(rf_s, rf_sem.at[1, 0])

    grad_ref[...] = jnp.sum(rf_s[...], axis=0)[:5]
    reduce_sent(*forward)
    wait_bytes(in_buf.at[pl.ds(0, 2 * ROWS - 1)], in_sem.at[0, 0])
    wait_bytes(un_buf.at[pl.ds(0, ROWS - 1)], un_sem.at[0, 0])
    wait_bytes(ro_s.at[pl.ds(0, ROWS - 1)], ro_sem.at[0, 0])
    wait_bytes(sum_buf.at[pl.ds(0, 2 * CHIPS - 1)], sum_sem.at[0, 0])
    wait_bytes(row_buf.at[pl.ds(0, 2 * ROWS - 1)], row_sem.at[0, 0])


def local(
    text_embeds,
    image_embeds,
    offsets,
    lengths,
    loss_mask,
    norm_gain,
    unembed_rows,
    gate_up,
    down_proj,
):
    width = text_embeds.shape[1]
    units = down_proj.shape[1]
    vmem = pl.BlockSpec(memory_space=pltpu.VMEM)
    smem = pl.BlockSpec(memory_space=pltpu.SMEM)
    anywhere = pl.BlockSpec(memory_space=pl.ANY)
    sems = pltpu.SemaphoreType.DMA

    def half(*shape):
        return pltpu.VMEM(shape, BF16)

    def full(*shape):
        return pltpu.VMEM(shape, F32)

    loss, grad = pl.pallas_call(
        kernel,
        out_shape=(jax.ShapeDtypeStruct((1, 1), F32), jax.ShapeDtypeStruct((5, width), F32)),
        in_specs=[vmem, vmem, smem, smem, smem, vmem, vmem, anywhere, anywhere],
        out_specs=(vmem, vmem),
        scratch_shapes=[
            half(2, units, width),
            half(units, width),
            half(3, TILE, width),
            half(2 * ROWS, 16, width),
            half(ROWS, 16, width),
            half(SEQ * 4, width),
            half(TILES, 2, HALF, 2 * TILE),
            half(TILES, HALF, 2 * TILE),
            half(10, HALF, 2 * TILE),
            half(HALF, 2 * TILE),
            half(4, HALF, 2 * TILE),
            half(4, HALF, 2 * TILE),
            half(TILES, 2, HALF, TILE),
            half(TILES, 2, HALF, TILE),
            half(TILES, HALF, TILE),
            half(10, HALF, TILE),
            half(HALF, TILE),
            half(4, HALF, TILE),
            half(4, HALF, TILE),
            half(TILES, 2, HALF, 2 * TILE),
            full(HALF, TILE),
            full(HALF, TILE),
            half(ROWS, 16, width),
            half(ROWS, 16, width),
            half(ROWS, 16, width),
            full(16, width),
            full(2 * CHIPS, 2, 128),
            full(2 * ROWS, 4, 128),
            full(2 * ROWS, 8, width),
            full(ROWS, 8, width),
            sems((2,)),
            sems((2, 1)),
            sems((2, 1)),
            sems((2, TILES)),
            sems((2, 11)),
            sems((2, 4)),
            sems((2, 17)),
            sems((2, TILES)),
            sems((2, TILES)),
            sems((2, 11)),
            sems((2, 4)),
            sems((2, 17)),
            sems((2, TILES)),
            sems((2, 1)),
            sems((2, 1)),
            sems((2, 1)),
            sems((2, 1)),
            sems((2, 1)),
        ],
        compiler_params=pltpu.CompilerParams(
            collective_id=0, has_side_effects=True, vmem_limit_bytes=40 << 20
        ),
        name="dpo_block",
    )(
        text_embeds,
        image_embeds,
        offsets,
        lengths,
        loss_mask,
        norm_gain,
        unembed_rows[0],
        jnp.transpose(gate_up[0], (1, 2, 0)),
        down_proj[0],
    )
    return loss.reshape(()), grad


def solution(mesh):
    in_specs = (
        P("row", "col"),
        P(("mp", "row"), "col"),
        P(),
        P(),
        P("row"),
        P("mp", "col"),
        P("mp", "row", "col"),
        P("mp", "col", None, "row"),
        P("mp", "row", "col"),
    )
    out_specs = (P(), P(("mp", "row"), "col"))
    return jax.shard_map(local, mesh=mesh, in_specs=in_specs, out_specs=out_specs, check_vma=False)
```

time: 424 us -> 146 us (0.34)
  blocking collectives: 210 us -> 0 us
  Pallas kernels: 0 us -> 135 us
  waiting for transfers between devices: 121 us -> 0 us
  starting transfers between devices: 39.7 us -> 0 us
  local copies, waits for them, and re-layouts: 22.9 us -> 8.02 us
  between operations: 16.2 us -> 2.41 us
  other arithmetic: 7.08 us -> 0 us
  matrix products: 5.32 us -> 0 us
    all_to_all x3 -> x0, blocking collectives: 185 us -> none  [the longest x2 173 us: sum_at_owner(): lax.all_to_all(blocks, axis, split_axis=0, concat_axis=0, tiled=True)]
    pallas_call x0 -> x1, Pallas kernels: none -> 135 us  [local(): pl.pallas_call(kernel, out_shape=(jax.ShapeDtypeStruct((1, 1), F32), jax....]
    all_to_all x7 -> x0, waiting for transfers between devices: 101 us -> none  [the longest x5 84.1 us: from_everyone(): lax.all_to_all(jnp.broadcast_to(array[None], (peers, *array.shape)), axis...]
    all_to_all x7 -> x0, starting transfers between devices: 39.7 us -> none  [the longest x5 29.4 us: from_everyone(): lax.all_to_all(jnp.broadcast_to(array[None], (peers, *array.shape)), axis...]
    all_gather x1 -> x0, blocking collectives: 25.1 us -> none  [stacked_from(): blocks = lax.all_gather(blocks, axes[k])]
    all_gather x1 -> x0, waiting for transfers between devices: 20.5 us -> none  [stacked_from(): blocks = lax.all_gather(blocks, axes[k])]
    unnamed x20 -> x19, local copies, waits for them, and re-layouts: 1.13 us -> 8.02 us
    reshape x8 -> x0, local copies, waits for them, and re-layouts: 6.14 us -> none  [the longest x4 4.08 us: split_up(): array.reshape(*lengths[:dim], peers, lengths[dim] // peers, *lengths[dim...]
  transfers between devices with their start and end apart: 8 -> 0, of which waited for: 8 -> 0; matrix products, arithmetic and copies ran while one was open for 2% -> 0% of each run, Pallas kernels for 0% -> 0%
where the time goes in v1:
time: 146 us; the launch traced here: 145 us
  Pallas kernels  135 us (92%)
  local copies, waits for them, and re-layouts  8.02 us (5%)
  between operations  2.41 us (2%)
    pallas_call x1, Pallas kernels, local(): pl.pallas_call(kernel, out_shape=(jax.ShapeDtypeStruct((1, 1), F32), jax....  135 us
    unnamed x19, local copies, waits for them, and re-layouts  8.02 us

profile of v1, /device:TPU:1, one launch (start us, length us, event | category | flops | bytes accessed | tf_op | source)
XLA Modules:
  0.0 145.0 jit_solution(5903851470940944389)
XLA Ops:
  0.6 0.0 copy-start
  0.6 1.5 %copy-done = bf16[1,256,2,1848]{1,3,2,0:T(8,128)(2,1)S(1)} copy-done((bf16[1,256,2,1848]{1,3,2,0:T(8,128)(2,1)S(1)}, bf16[1,256,2,1848]{1,3,2,0:T(8,128)(2,1)}, u32[]{:S(2)}) %copy-start) | copy-done | bytes 1892376
  2.2 0.0 copy-start.1
  2.2 1.2 copy-done.1
  3.3 0.0 copy-start.2
  3.3 0.7 copy-done.2
  4.0 0.0 copy-start.3
  4.0 0.7 copy-done.3
  4.7 0.0 copy-start.4
  4.7 0.7 copy-done.4
  5.4 0.0 copy-start.5
  5.4 0.7 copy-done.5
  6.1 0.0 copy-start.6
  6.1 0.7 copy-done.6
  6.8 0.0 copy-start.7
  6.8 0.7 copy-done.7
  7.4 0.0 copy-start.8
  7.4 0.7 copy-done.8
  8.1 134.6 %dpo_block.1 = (f32[1,1]{1,0:T(1,128)}, f32[5,256]{1,0:T(8,128)S(1)}) custom-call(bf16[10,256]{1,0:T(8,128)(2,1)S(1)} %copy-done.2, bf16[2,256]{1,0:T(2,128)(2,1)S(1)} %copy-done.4, s32[4]{0:T(128)S(1)} %copy-done.6, s32[4]{0:T(128)S(1)} %copy-done.7, s32[10]{0:T(128)S(1)} %copy-done.8, bf16[1,256]{1,0:T(2,128)(2,1)S(1)} %copy-done.5, ...), custom_call_target="tpu_custom_call" | custom-call | tf_op jit(solution)/shard_map/dpo_block/pallas_call | solution.py:570
  143.3 0.6 copy.14
Async XLA Ops:
  0.6 1.5 %copy-start = (bf16[1,256,2,1848]{1,3,2,0:T(8,128)(2,1)S(1)}, bf16[1,256,2,1848]{1,3,2,0:T(8,128)(2,1)}, u32[]{:S(2)}) copy-start(bf16[1,256,2,1848]{1,3,2,0:T(8,128)(2,1)} %param.16) | copy-start | bytes 5677060
  2.2 1.2 copy-start.1
  3.3 0.7 copy-start.2
  4.0 0.7 copy-start.3
  4.7 0.7 copy-start.4
  5.4 0.7 copy-start.5
  6.1 0.7 copy-start.6
  6.8 0.7 copy-start.7
  7.4 0.7 copy-start.8

commit v2 on v1

v2 whole, which is shorter than its diff:
```python
import jax
import jax.numpy as jnp
from jax import lax
from jax.experimental import pallas as pl
from jax.experimental.pallas import tpu as pltpu
from jax.sharding import PartitionSpec as P

D = 8192
SEQ = 40
IMG = 16
ROWS = 16
CHIPS = 16
OWN = 10
HALF = 80
TILE = 128
TILES = 15
LAST = 56
BETA = 0.1
EPS = 1e-06
MESH = pl.DeviceIdType.MESH
LEADERS = (0, 3, -3, 6, -6)
F32 = jnp.float32
BF16 = jnp.bfloat16


def iota(shape, dim):
    return lax.broadcasted_iota(jnp.int32, shape, dim)


def dot(a, b, precision=None):
    return jnp.dot(a, b, preferred_element_type=F32, precision=precision)


def dot_t(a, b):
    return lax.dot_general(a, b, (((1,), (1,)), ((), ())), preferred_element_type=F32)


def kernel(
    text_in,
    image_in,
    offsets_in,
    lengths_in,
    mask_in,
    gain_in,
    unembed_in,
    gate_up_ref,
    down_ref,
    loss_ref,
    grad_ref,
    text_ref,
    image_ref,
    offsets_ref,
    lengths_ref,
    mask_ref,
    gain_ref,
    unembed_ref,
    w_s,
    d_s,
    wt_s,
    dt_s,
    tx_buf,
    im_buf,
    un_buf,
    x_s,
    p_s,
    px_s,
    l1_s,
    lx_s,
    s_s,
    l2_s,
    h_s,
    q_s,
    qx_s,
    m1_s,
    mx_s,
    t_s,
    m2_s,
    ab_s,
    g_s,
    so_s,
    ro_s,
    res_buf,
    res_s,
    sum_s,
    pair_s,
    sum_buf,
    row_buf,
    dr_s,
    sf_s,
    rf_s,
    spread_s,
    compact_s,
    owner_s,
    w_sem,
    tx_sem,
    im_sem,
    un_sem,
    fx_sem,
    f1_sem,
    f2_sem,
    hz_sem,
    hc_sem,
    az_sem,
    ac_sem,
    bx_sem,
    b1_sem,
    b2_sem,
    gz_sem,
    gc_sem,
    ro_sem,
    res_sem,
    pair_sem,
    sum_sem,
    row_sem,
    rf_sem,
):
    mp = lax.axis_index("mp")
    row = lax.axis_index("row")
    col = lax.axis_index("col")
    plane = mp * ROWS + row
    z = lax.div(col, 2)
    core = lax.rem(col, 2)

    def chip(offset):
        return lax.rem(z + offset + 2 * CHIPS, CHIPS)

    def at_chip(where):
        return {"col": 2 * where + core}

    def plane_id(index):
        return {"mp": lax.div(index, ROWS), "row": lax.rem(index, ROWS)}

    partner = {"col": 2 * z + 1 - core}

    def remote(src, dst, sems, index, device):
        return pltpu.make_async_remote_copy(
            src_ref=src,
            dst_ref=dst,
            send_sem=sems.at[0, index],
            recv_sem=sems.at[1, index],
            device_id=device,
            device_id_type=MESH,
        )

    def wait_bytes(ref, sem):
        pltpu.make_async_copy(ref, ref, sem).wait()

    copies = [
        pltpu.make_async_copy(src, dst, w_sem.at[n])
        for n, (src, dst) in enumerate(
            (
                (gate_up_ref, w_s),
                (down_ref, d_s),
                (text_in, text_ref),
                (image_in, image_ref),
                (unembed_in, unembed_ref),
                (gain_in, gain_ref),
                (offsets_in, offsets_ref),
                (lengths_in, lengths_ref),
                (mask_in, mask_ref),
            )
        )
    ]
    for copy in copies[2:]:
        copy.start()
    for copy in copies[:2]:
        copy.start()

    barrier = pltpu.get_barrier_semaphore()

    def greet_plane(d, carry):
        other = lax.rem(plane + d, 2 * ROWS)
        pl.semaphore_signal(barrier, inc=1, device_id=plane_id(other), device_id_type=MESH)
        return carry

    def greet_col(d, carry):
        pl.semaphore_signal(barrier, inc=1, device_id=at_chip(chip(d)), device_id_type=MESH)
        return carry

    lax.fori_loop(1, CHIPS, greet_col, 0)
    lax.fori_loop(1, 2 * ROWS, greet_plane, 0)
    pl.semaphore_signal(barrier, inc=1, device_id=partner, device_id_type=MESH)

    for copy in copies[2:]:
        copy.wait()
    width = text_ref.shape[1]

    zeros = jnp.zeros((6, width), F32)
    tx_buf[row] = jnp.concatenate([text_ref[...].astype(F32), zeros], axis=0).astype(BF16)
    im_buf[plane] = image_ref[...]
    own_unembed = jnp.concatenate([unembed_ref[...].astype(F32), zeros], axis=0)
    un_buf[row] = own_unembed.astype(BF16)
    gain = gain_ref[...].astype(F32)

    tokens = SEQ * 4
    token = iota((tokens, 1), 0)
    position = lax.rem(token, SEQ)
    seq_id = lax.div(token, SEQ)
    first = jnp.where(
        seq_id == 0,
        offsets_ref[0],
        jnp.where(seq_id == 1, offsets_ref[1], jnp.where(seq_id == 2, offsets_ref[2], offsets_ref[3])),
    )
    inside = (position >= first) & (position < first + IMG)
    token_slot = lax.div(token, OWN) * 16 + lax.rem(token, OWN)
    from_text = jnp.where(inside, -1, token_slot)
    from_image = jnp.where(inside, seq_id * IMG + position - first, -1)
    pick_text = (iota((tokens, ROWS * 16), 1) == from_text).astype(BF16)
    pick_image = (iota((tokens, 4 * IMG), 1) == from_image).astype(BF16)

    slot = iota((ROWS * 16, 1), 0)
    slot_token = jnp.where((slot & 15) < OWN, lax.shift_right_arithmetic(slot, 4) * OWN + (slot & 15), -1)
    spread_s[...] = (iota((ROWS * 16, tokens), 1) == slot_token).astype(BF16)
    compact_s[...] = (iota((tokens, ROWS * 16), 1) == token_slot).astype(BF16)
    owner_token = jnp.where((slot & 7) < 5, lax.shift_right_arithmetic(slot, 3) * 5 + (slot & 7), -1)
    owner_s[...] = (iota((ROWS * 16, tokens), 1) == owner_token).astype(BF16)

    for copy in copies[:2]:
        copy.wait()

    def lay_tile(j, carry):
        rows = pl.ds(pl.multiple_of(j * TILE, TILE), TILE)
        wt_s[j, :TILE] = w_s[0, rows]
        wt_s[j, TILE:] = w_s[1, rows]
        dt_s[j] = d_s[rows]
        return carry

    lax.fori_loop(0, TILES - 1, lay_tile, 0)
    last = TILES - 1
    wt_s[last:] = jnp.zeros((2, 2 * TILE, width), BF16)
    dt_s[last:] = jnp.zeros((2, TILE, width), BF16)
    wt_s[last, :LAST] = w_s[0, last * TILE :]
    wt_s[last, TILE : TILE + LAST] = w_s[1, last * TILE :]
    dt_s[last, :LAST] = d_s[last * TILE :]

    pl.semaphore_wait(barrier, 2 * ROWS - 1 + CHIPS)

    def to_plane(make):
        def send(d, carry):
            make(lax.rem(plane + 1 + lax.rem(d + 6, 2 * ROWS - 1), 2 * ROWS)).start()
            return carry

        lax.fori_loop(0, 2 * ROWS - 1, send, 0)

    def to_row(make):
        def send(d, carry):
            make(lax.rem(row + 1 + lax.rem(d + 5, ROWS - 1), ROWS)).start()
            return carry

        lax.fori_loop(0, ROWS - 1, send, 0)

    def all_but_one(ref):
        return ref.at[pl.ds(0, ref.shape[0] - 1)]

    to_row(lambda o: remote(tx_buf.at[row], tx_buf.at[row], tx_sem, 0, {"row": o}))
    to_plane(lambda o: remote(im_buf.at[plane], im_buf.at[plane], im_sem, 0, plane_id(o)))
    wait_bytes(all_but_one(tx_buf), tx_sem.at[1, 0])
    texts = dot(pick_text, tx_buf[...].reshape(ROWS * 16, width))
    wait_bytes(all_but_one(im_buf), im_sem.at[1, 0])
    images = jnp.concatenate([im_buf[i].astype(F32) for i in range(2 * ROWS)], axis=0).astype(BF16)
    x_s[...] = (texts + dot(pick_image, images)).astype(BF16)

    far_group = (5, 7, -5, -7, 8, 6, -6)
    mid_group = (2, 4, -2, -4, 3, -3)
    near_group = (1, -1, 0)

    def leader_of(o):
        lead = min((l for l in LEADERS if abs(l - o) == 1), default=None, key=abs)
        k = LEADERS.index(lead)
        return lead, 2 * k + (0 if o < lead else 1)

    def reduce(partial, p, px, l1, lx, s, l2, sx, s1, s2, deep, between=lambda: None):
        def compute(group):
            for o in group:
                j = chip(-o)
                p[j] = partial(j).astype(BF16).reshape(2, HALF, p.shape[3])
                remote(p.at[j, 1 - core], px.at[j], sx, j, partner).start()

        def pair(j):
            remote(p.at[j, 1 - core], px.at[j], sx, j, partner).wait_recv()
            return p[j, core].astype(F32) + px[j].astype(F32)

        def first_sums(group):
            for o in group:
                if o in LEADERS:
                    continue
                j = chip(-o)
                if o == 8:
                    dst, index, target = lx, 10, chip(4 * core - 2)
                else:
                    lead, index = leader_of(o)
                    dst, target = l1.at[index], chip(lead - o)

                @pl.when(j != TILES)
                def _(j=j, dst=dst, index=index, target=target):
                    p[j, core] = pair(j).astype(BF16)
                    remote(p.at[j, core], dst, s1, index, at_chip(target)).start()

        def arrived(ref, sems, index):
            remote(ref, ref, sems, index, partner).wait_recv()
            return ref[...].astype(F32)

        compute(far_group)
        compute(mid_group)
        first_sums(far_group)
        compute(near_group)
        first_sums(mid_group)
        first_sums(near_group)
        between()
        for k in (3, 4, 1, 2):
            lead = LEADERS[k]
            j = chip(-lead)

            @pl.when(j != TILES)
            def _(k=k, lead=lead, j=j):
                total = pair(j)
                for slot in (2 * k, 2 * k + 1):
                    total = total + arrived(l1.at[slot], s1, slot)
                target = j
                if abs(lead) == 6:
                    extra = core == (0 if lead == 6 else 1)

                    @pl.when(extra)
                    def _():
                        s[k - 1] = (total + arrived(lx, s1, 10)).astype(BF16)

                    @pl.when(jnp.logical_not(extra))
                    def _():
                        s[k - 1] = total.astype(BF16)

                    if deep:
                        target = chip(-lead // 2)
                else:
                    if deep:
                        total = total + arrived(l2.at[k + 1], s2, k + 1)
                    s[k - 1] = total.astype(BF16)
                remote(s.at[k - 1], l2.at[k - 1], s2, k - 1, at_chip(target)).start()

        def final():
            total = pair(z)
            for slot in (0, 1):
                total = total + arrived(l1.at[slot], s1, slot)
            for k in range(2 if deep else 4):
                total = total + arrived(l2.at[k], s2, k)
            return total

        def sent():
            remote(p.at[TILES, 1 - core], px.at[TILES], sx, TILES, partner).wait_recv()
            for j in range(TILES + 1):
                remote(p.at[j, 1 - core], px.at[j], sx, j, partner).wait_send()
            for o in range(-7, 9):
                if o in LEADERS:
                    continue
                index = 10 if o == 8 else leader_of(o)[1]

                @pl.when(chip(-o) != TILES)
                def _(index=index):
                    remote(lx, lx, s1, index, partner).wait_send()

            for k in range(1, 5):

                @pl.when(chip(-LEADERS[k]) != TILES)
                def _(k=k):
                    remote(lx, lx, s2, k - 1, partner).wait_send()

        return final, sent

    mine = z != TILES

    def gather(g, sz, sc):
        sends = []

        def send(block, by, o, came, relay=None):
            n = len(sends)
            pltpu.make_async_remote_copy(
                src_ref=g.at[block, core],
                dst_ref=g.at[block, core],
                send_sem=sz.at[0, n],
                recv_sem=sz.at[1, o + 7],
                device_id=at_chip(chip(by)),
                device_id_type=MESH,
            ).start()
            sends.append((n, came, relay))

        def across(block):
            remote(g.at[block, core], g.at[block, core], sc, block, partner).start()

        def arrived(block, o):
            pltpu.make_async_remote_copy(
                src_ref=g.at[block, core],
                dst_ref=g.at[block, core],
                send_sem=sz.at[0, 0],
                recv_sem=sz.at[1, o + 7],
                device_id=partner,
                device_id_type=MESH,
            ).wait_recv()

        def begin():
            @pl.when(mine)
            def _():
                for o in (6, -6, 3, -3, 1, -1):
                    send(z, o, o, 0)
                across(z)

        def take(offsets):
            for o in offsets:
                block = chip(-o)
                there = block != TILES
                relay = 0 if o == 6 else 1

                @pl.when(there)
                def _(o=o, block=block, relay=relay):
                    arrived(block, o)
                    if o in LEADERS:
                        if abs(o) == 6:

                            @pl.when(core == relay)
                            def _():
                                send(block, 2 if o == 6 else -2, 8, o, relay)

                        send(block, 1, o + 1, o)
                        send(block, -1, o - 1, o)
                    across(block)

        def end():
            for j in range(TILES):
                remote(g.at[j, core], g.at[j, core], sc, j, partner).wait()

        def sent():
            for n, came, relay in sends:
                when = chip(-came) != TILES
                if relay is not None:
                    when = when & (core == relay)

                @pl.when(when)
                def _(n=n):
                    remote(g.at[0, 0], g.at[0, 0], sz, n, partner).wait_send()

        return begin, take, end, sent

    leads = (3, -3, 6, -6)
    others = (1, -1, 2, -2, 4, -4, 5, -5, 7, -7, 8)

    x = x_s[...]
    forward_final, forward_sent = reduce(
        lambda j: dot_t(x, wt_s[j]), p_s, px_s, l1_s, lx_s, s_s, l2_s, fx_sem, f1_sem, f2_sem, True
    )
    h_begin, h_take, h_end, h_sent = gather(h_s, hz_sem, hc_sem)

    @pl.when(mine)
    def _():
        pre = forward_final()
        gate = pre[:, :TILE]
        up = pre[:, TILE:]
        sig = jax.nn.sigmoid(gate)
        silu = gate * sig
        h_s[z, core] = (silu * up).astype(BF16)
        ab_s[z, core] = jnp.concatenate([up * sig * (1.0 + gate * (1.0 - sig)), silu], axis=1).astype(BF16)

    h_begin()
    h_take((1, -1) + leads)

    @pl.when(mp == 0)
    def _():
        to_row(lambda o: remote(un_buf.at[row], un_buf.at[row], un_sem, 0, {"row": o}))

    h_take(others[2:])
    h_end()

    def hidden(j):
        return h_s[j].reshape(2 * HALF, TILE)

    out = dot(hidden(TILES - 1), dt_s[TILES - 1])
    for j in range(0, TILES - 1, 2):
        both = jnp.concatenate([hidden(j), hidden(j + 1)], axis=1)
        out = out + dot(both, dt_s[j : j + 2].reshape(2 * TILE, width))
    so_s[...] = dot(spread_s[...], out.astype(BF16)).astype(BF16).reshape(so_s.shape)
    to_row(lambda o: remote(so_s.at[o], ro_s.at[row], ro_sem, 0, {"row": o}))
    ro_s[row] = so_s[row]
    a_begin, a_take, a_end, a_sent = gather(ab_s, az_sem, ac_sem)

    @pl.when(mp == 0)
    def _():
        a_begin()

    own_row = iota((16, tokens), 0)
    own_pick = ((iota((16, tokens), 1) == row * OWN + own_row) & (own_row < OWN)).astype(BF16)
    own_rows = dot(own_pick, x)
    coeff = own_unembed * gain
    wait_bytes(all_but_one(ro_s), ro_sem.at[1, 0])
    residual = own_rows + jnp.sum(ro_s[...].astype(F32), axis=0)
    res_s[...] = residual

    square = (iota((16, 128), 0) == iota((16, 128), 1)).astype(F32)

    def as_row(values):
        return jnp.sum(values * square, axis=0, keepdims=True)

    def as_column(values):
        return jnp.sum(values * square, axis=1, keepdims=True)

    sum_s[...] = jnp.concatenate(
        [
            as_row(jnp.sum(residual * residual, axis=1, keepdims=True)),
            as_row(jnp.sum(residual * coeff, axis=1, keepdims=True)),
        ],
        axis=0,
    )
    to_partner = remote(sum_s, pair_s, pair_sem, 0, partner)
    to_partner.start()
    res_buf[row] = residual.astype(BF16)
    lane = iota((1, 128), 1)
    masked = jnp.zeros((1, 128), jnp.int32)
    for t in range(OWN):
        masked = jnp.where(lane == t, mask_ref[t], masked)
    place = lax.rem(row, 4) * OWN + lane
    scored = ((place < lengths_ref[lax.div(row, 4)]) & (masked == 1) & (lane < OWN)).astype(F32)
    to_partner.wait_recv()
    sum_buf[z] = sum_s[...] + pair_s[...]

    def send_sums(d, carry):
        other = lax.rem(z + 1 + lax.rem(d + 5, CHIPS - 1), CHIPS)
        remote(sum_buf.at[z], sum_buf.at[z], sum_sem, 0, at_chip(other)).start()
        return carry

    lax.fori_loop(0, CHIPS - 1, send_sums, 0)

    @pl.when(mp == 0)
    def _():
        to_row(lambda o: remote(res_buf.at[row], res_buf.at[row], res_sem, 0, {"row": o}))

    wait_bytes(all_but_one(sum_buf), sum_sem.at[1, 0])
    totals = jnp.sum(sum_buf[...], axis=0)
    squares = totals[0:1]
    cross = totals[1:2]
    inv_rms = lax.rsqrt(squares / D + EPS)
    by_coeff = scored * inv_rms
    by_residual = scored * (cross * inv_rms * inv_rms * inv_rms / D)
    row_buf[plane] = jnp.concatenate(
        [scored * (cross * inv_rms), by_coeff, by_residual, jnp.zeros((1, 128), F32)], axis=0
    )
    to_plane(lambda o: remote(row_buf.at[plane], row_buf.at[plane], row_sem, 0, plane_id(o)))

    @pl.when(mp == 0)
    def _():
        a_take(leads)

    wait_bytes(all_but_one(row_buf), row_sem.at[1, 0])
    margins = []
    for q in range(2):
        acc = jnp.zeros((1, 128), F32)
        for r in range(8):
            policy = row_buf[8 * q + r][0:1]
            frozen = row_buf[ROWS + 8 * q + r][0:1]
            acc = acc + (policy - frozen if r < 4 else frozen - policy)
        margins.append(jnp.sum(acc, axis=1, keepdims=True))
    logits = [-BETA * m for m in margins]
    losses = [jnp.maximum(v, 0.0) + jnp.log1p(jnp.exp(-jnp.abs(v))) for v in logits]
    loss_ref[...] = (losses[0] + losses[1]) * 0.5
    dmargin = [-BETA * jax.nn.sigmoid(v) * 0.5 for v in logits]

    def two_parts(values):
        high = values.astype(BF16)
        return high, (values - high.astype(F32)).astype(BF16)

    @pl.when(mp == 0)
    def _():
        wait_bytes(all_but_one(un_buf), un_sem.at[1, 0])
        wait_bytes(all_but_one(res_buf), res_sem.at[1, 0])
        rows = []
        for r in range(ROWS):
            grad = dmargin[r // 8] if (r // 4) % 2 == 0 else -dmargin[r // 8]
            terms = row_buf[r]
            rows.append(
                (
                    (as_column(terms[1:2]) * grad) * (un_buf[r].astype(F32) * gain)
                    - (as_column(terms[2:3]) * grad) * res_buf[r].astype(F32)
                ).astype(BF16)
            )
        dy = dot(compact_s[...], jnp.concatenate(rows, axis=0)).astype(BF16)

        def between():
            a_take(others)
            first_pair = jnp.where(lax.div(row, 8) == 0, dmargin[0], dmargin[1])
            own_grad = jnp.where(lax.rem(lax.div(row, 4), 2) == 0, first_pair, -first_pair)
            dresidual = (as_column(by_coeff) * own_grad) * coeff - (
                as_column(by_residual) * own_grad
            ) * res_s[...]
            back_slot = iota((tokens, 16), 1)
            back = ((iota((tokens, 16), 0) == row * OWN + back_slot) & (back_slot < OWN)).astype(BF16)
            high, low = two_parts(dresidual)
            dr_s[...] = dot(back, high) + dot(back, low)

        backward_final, backward_sent = reduce(
            lambda j: dot_t(dy, dt_s[j]),
            q_s,
            qx_s,
            m1_s,
            mx_s,
            t_s,
            m2_s,
            bx_sem,
            b1_sem,
            b2_sem,
            False,
            between,
        )
        g_begin, g_take, g_end, g_sent = gather(g_s, gz_sem, gc_sem)

        @pl.when(mine)
        def _():
            g_s[z, core] = backward_final().astype(BF16)

        g_begin()
        g_take((1, -1) + leads)
        a_end()
        g_take(others[2:])
        g_end()
        total = dr_s[...]
        for j in range(TILES):
            dhidden = g_s[j].reshape(2 * HALF, TILE).astype(F32)
            factors = ab_s[j].reshape(2 * HALF, 2 * TILE).astype(F32)
            pre_grad = (jnp.concatenate([dhidden, dhidden], axis=1) * factors).astype(BF16)
            total = total + dot(pre_grad, wt_s[j])
        high, low = two_parts(total)
        by_owner = owner_s[...]
        sf_s[...] = (dot(by_owner, high) + dot(by_owner, low)).reshape(sf_s.shape)
        to_plane(lambda o: remote(sf_s.at[o], rf_s.at[row], rf_sem, 0, plane_id(o)))
        rf_s[row] = sf_s[row]
        backward_sent()
        a_sent()
        g_sent()
        wait_bytes(all_but_one(un_buf), un_sem.at[0, 0])
        wait_bytes(all_but_one(res_buf), res_sem.at[0, 0])
        wait_bytes(all_but_one(rf_s), rf_sem.at[1, 0])
        wait_bytes(all_but_one(sf_s), rf_sem.at[0, 0])

    @pl.when(mp == 1)
    def _():
        wait_bytes(rf_s, rf_sem.at[1, 0])

    grad_ref[...] = jnp.sum(rf_s[...], axis=0)[:5]
    forward_sent()
    h_sent()
    to_partner.wait_send()
    wait_bytes(all_but_one(tx_buf), tx_sem.at[0, 0])
    wait_bytes(all_but_one(im_buf), im_sem.at[0, 0])
    wait_bytes(all_but_one(ro_s), ro_sem.at[0, 0])
    wait_bytes(all_but_one(sum_buf), sum_sem.at[0, 0])
    wait_bytes(all_but_one(row_buf), row_sem.at[0, 0])


def local(
    text_embeds,
    image_embeds,
    offsets,
    lengths,
    loss_mask,
    norm_gain,
    unembed_rows,
    gate_up,
    down_proj,
):
    width = text_embeds.shape[1]
    units = down_proj.shape[1]
    vmem = pl.BlockSpec(memory_space=pltpu.VMEM)
    anywhere = pl.BlockSpec(memory_space=pl.ANY)
    sems = pltpu.SemaphoreType.DMA

    def half(*shape):
        return pltpu.VMEM(shape, BF16)

    def full(*shape):
        return pltpu.VMEM(shape, F32)

    def tree(units):
        return [
            half(TILES + 1, 2, HALF, units),
            half(TILES + 1, HALF, units),
            half(10, HALF, units),
            half(HALF, units),
            half(4, HALF, units),
            half(4, HALF, units),
        ]

    loss, grad = pl.pallas_call(
        kernel,
        out_shape=(jax.ShapeDtypeStruct((1, 1), F32), jax.ShapeDtypeStruct((5, width), F32)),
        in_specs=[anywhere] * 9,
        out_specs=(vmem, vmem),
        scratch_shapes=[
            half(*text_embeds.shape),
            half(*image_embeds.shape),
            pltpu.SMEM(offsets.shape, jnp.int32),
            pltpu.SMEM(lengths.shape, jnp.int32),
            pltpu.SMEM(loss_mask.shape, jnp.int32),
            half(*norm_gain.shape),
            half(*unembed_rows.shape[1:]),
            half(2, units, width),
            half(units, width),
            half(TILES + 1, 2 * TILE, width),
            half(TILES + 1, TILE, width),
            half(ROWS, 16, width),
            half(2 * ROWS, *image_embeds.shape),
            half(ROWS, 16, width),
            half(SEQ * 4, width),
            *tree(2 * TILE),
            half(TILES, 2, HALF, TILE),
            *tree(TILE),
            half(TILES + 1, 2, HALF, 2 * TILE),
            half(TILES, 2, HALF, TILE),
            half(ROWS, 16, width),
            half(ROWS, 16, width),
            half(ROWS, 16, width),
            full(16, width),
            full(2, 128),
            full(2, 128),
            full(CHIPS, 2, 128),
            full(2 * ROWS, 4, 128),
            full(SEQ * 4, width),
            full(2 * ROWS, 8, width),
            full(ROWS, 8, width),
            half(ROWS * 16, SEQ * 4),
            half(SEQ * 4, ROWS * 16),
            half(ROWS * 16, SEQ * 4),
            sems((9,)),
            sems((2, 1)),
            sems((2, 1)),
            sems((2, 1)),
            sems((2, TILES + 1)),
            sems((2, 11)),
            sems((2, 4)),
            sems((2, 17)),
            sems((2, TILES)),
            sems((2, 17)),
            sems((2, TILES)),
            sems((2, TILES + 1)),
            sems((2, 11)),
            sems((2, 4)),
            sems((2, 17)),
            sems((2, TILES)),
            *[sems((2, 1))] * 6,
        ],
        compiler_params=pltpu.CompilerParams(
            collective_id=0, has_side_effects=True, vmem_limit_bytes=60 << 20
        ),
        name="dpo_block",
    )(
        text_embeds,
        image_embeds,
        offsets,
        lengths,
        loss_mask,
        norm_gain,
        unembed_rows[0],
        jnp.transpose(gate_up[0], (1, 2, 0)),
        down_proj[0],
    )
    return loss.reshape(()), grad


def solution(mesh):
    in_specs = (
        P("row", "col"),
        P(("mp", "row"), "col"),
        P(),
        P(),
        P("row"),
        P("mp", "col"),
        P("mp", "row", "col"),
        P("mp", "col", None, "row"),
        P("mp", "row", "col"),
    )
    out_specs = (P(), P(("mp", "row"), "col"))
    return jax.shard_map(local, mesh=mesh, in_specs=in_specs, out_specs=out_specs, check_vma=False)
```

time: 146 us -> 129 us (0.88)
  Pallas kernels: 135 us -> 125 us
  local copies, waits for them, and re-layouts: 8.02 us -> 1.3 us
    pallas_call x1, Pallas kernels: 135 us -> 125 us  [local(): pl.pallas_call(kernel, out_shape=(jax.ShapeDtypeStruct((1, 1), F32), jax....]
    unnamed x19 -> x1, local copies, waits for them, and re-layouts: 8.02 us -> 1.3 us
where the time goes in v2:
time: 129 us
  Pallas kernels  125 us (97%)
  between operations  2.4 us (2%)
  local copies, waits for them, and re-layouts  1.3 us (1%)
    pallas_call x1, Pallas kernels, local(): pl.pallas_call(kernel, out_shape=(jax.ShapeDtypeStruct((1, 1), F32), jax....  125 us

profile of v2, /device:TPU:1, one launch (start us, length us, event | category | flops | bytes accessed | tf_op | source)
XLA Modules:
  0.0 129.0 jit_solution(4731005351568110137)
XLA Ops:
  0.6 125.3 %dpo_block.1 = (f32[1,1]{1,0:T(1,128)}, f32[5,256]{1,0:T(8,128)}) custom-call(bf16[10,256]{1,0:T(8,128)(2,1)} %text_in.1, bf16[2,256]{1,0:T(2,128)(2,1)} %image_in.1, s32[4]{0:T(128)} %offsets_in.1, s32[4]{0:T(128)} %lengths_in.1, s32[10]{0:T(128)} %mask_in.1, bf16[1,256]{1,0:T(2,128)(2,1)} %gain_in.1, bf16[10,256]{1,0:T(8,128)(2,1)} %bitcast.8, ...), custom_call_target="tpu_custom_call" | custom-call | tf_op jit(solution)/shard_map/dpo_block/pallas_call | solution.py:686
  126.6 1.3 %copy.14 = f32[5,256]{1,0:T(8,128)} copy(f32[5,256]{1,0:T(8,128)} %get-tuple-element.9) | data formatting | bytes 10240

commit v3 on v2

--- a/solution.py
+++ b/solution.py
@@ -186,12 +186,40 @@
     width = text_ref.shape[1]
 
     zeros = jnp.zeros((6, width), F32)
-    tx_buf[row] = jnp.concatenate([text_ref[...].astype(F32), zeros], axis=0).astype(BF16)
-    im_buf[plane] = image_ref[...]
+    tx_buf[row] = jnp.concatenate(
+        [text_ref[...].astype(F32), image_ref[...].astype(F32), zeros[:4]], axis=0
+    ).astype(BF16)
     own_unembed = jnp.concatenate([unembed_ref[...].astype(F32), zeros], axis=0)
     un_buf[row] = own_unembed.astype(BF16)
     gain = gain_ref[...].astype(F32)
 
+    pl.semaphore_wait(barrier, 2 * ROWS - 1 + CHIPS)
+
+    def to_plane(make):
+        def send(d, carry):
+            make(lax.rem(plane + 1 + lax.rem(d + 6, 2 * ROWS - 1), 2 * ROWS)).start()
+            return carry
+
+        lax.fori_loop(0, 2 * ROWS - 1, send, 0)
+
+    def to_row(make):
+        def send(d, carry):
+            make(lax.rem(row + 1 + lax.rem(d + 5, ROWS - 1), ROWS)).start()
+            return carry
+
+        lax.fori_loop(0, ROWS - 1, send, 0)
+
+    def all_but_one(ref):
+        return ref.at[pl.ds(0, ref.shape[0] - 1)]
+
+    to_row(lambda o: remote(tx_buf.at[row], tx_buf.at[row], tx_sem, 0, {"row": o}))
+
+    def send_image(d, carry):
+        other = {"mp": 1 - mp, "row": lax.rem(row + 6 + d, ROWS)}
+        remote(image_ref, im_buf.at[row], im_sem, 0, other).start()
+        return carry
+
+    lax.fori_loop(0, ROWS, send_image, 0)
     tokens = SEQ * 4
     token = iota((tokens, 1), 0)
     position = lax.rem(token, SEQ)
@@ -203,17 +231,14 @@
     )
     inside = (position >= first) & (position < first + IMG)
     token_slot = lax.div(token, OWN) * 16 + lax.rem(token, OWN)
-    from_text = jnp.where(inside, -1, token_slot)
-    from_image = jnp.where(inside, seq_id * IMG + position - first, -1)
+    image_row = seq_id * IMG + position - first
+    in_half = image_row - mp * (2 * IMG)
+    near = (in_half >= 0) & (in_half < 2 * IMG)
+    with_text = lax.shift_right_arithmetic(in_half, 1) * 16 + OWN + (in_half & 1)
+    from_text = jnp.where(inside, jnp.where(near, with_text, -1), token_slot)
+    from_image = jnp.where(inside & jnp.logical_not(near), image_row - (1 - mp) * (2 * IMG), -1)
     pick_text = (iota((tokens, ROWS * 16), 1) == from_text).astype(BF16)
-    pick_image = (iota((tokens, 4 * IMG), 1) == from_image).astype(BF16)
-
-    slot = iota((ROWS * 16, 1), 0)
-    slot_token = jnp.where((slot & 15) < OWN, lax.shift_right_arithmetic(slot, 4) * OWN + (slot & 15), -1)
-    spread_s[...] = (iota((ROWS * 16, tokens), 1) == slot_token).astype(BF16)
-    compact_s[...] = (iota((tokens, ROWS * 16), 1) == token_slot).astype(BF16)
-    owner_token = jnp.where((slot & 7) < 5, lax.shift_right_arithmetic(slot, 3) * 5 + (slot & 7), -1)
-    owner_s[...] = (iota((ROWS * 16, tokens), 1) == owner_token).astype(BF16)
+    pick_image = (iota((tokens, 2 * IMG), 1) == from_image).astype(BF16)
 
     for copy in copies[:2]:
         copy.wait()
@@ -233,36 +258,16 @@
     wt_s[last, TILE : TILE + LAST] = w_s[1, last * TILE :]
     dt_s[last, :LAST] = d_s[last * TILE :]
 
-    pl.semaphore_wait(barrier, 2 * ROWS - 1 + CHIPS)
-
-    def to_plane(make):
-        def send(d, carry):
-            make(lax.rem(plane + 1 + lax.rem(d + 6, 2 * ROWS - 1), 2 * ROWS)).start()
-            return carry
-
-        lax.fori_loop(0, 2 * ROWS - 1, send, 0)
-
-    def to_row(make):
-        def send(d, carry):
-            make(lax.rem(row + 1 + lax.rem(d + 5, ROWS - 1), ROWS)).start()
-            return carry
-
-        lax.fori_loop(0, ROWS - 1, send, 0)
-
-    def all_but_one(ref):
-        return ref.at[pl.ds(0, ref.shape[0] - 1)]
-
-    to_row(lambda o: remote(tx_buf.at[row], tx_buf.at[row], tx_sem, 0, {"row": o}))
-    to_plane(lambda o: remote(im_buf.at[plane], im_buf.at[plane], im_sem, 0, plane_id(o)))
     wait_bytes(all_but_one(tx_buf), tx_sem.at[1, 0])
     texts = dot(pick_text, tx_buf[...].reshape(ROWS * 16, width))
-    wait_bytes(all_but_one(im_buf), im_sem.at[1, 0])
-    images = jnp.concatenate([im_buf[i].astype(F32) for i in range(2 * ROWS)], axis=0).astype(BF16)
+    wait_bytes(im_buf, im_sem.at[1, 0])
+    images = jnp.concatenate([im_buf[i].astype(F32) for i in range(ROWS)], axis=0).astype(BF16)
     x_s[...] = (texts + dot(pick_image, images)).astype(BF16)
 
     far_group = (5, 7, -5, -7, 8, 6, -6)
     mid_group = (2, 4, -2, -4, 3, -3)
     near_group = (1, -1, 0)
+    order = far_group + mid_group + near_group
 
     def leader_of(o):
         lead = min((l for l in LEADERS if abs(l - o) == 1), default=None, key=abs)
@@ -272,13 +277,14 @@
     def reduce(partial, p, px, l1, lx, s, l2, sx, s1, s2, deep, between=lambda: None):
         def compute(group):
             for o in group:
-                j = chip(-o)
-                p[j] = partial(j).astype(BF16).reshape(2, HALF, p.shape[3])
-                remote(p.at[j, 1 - core], px.at[j], sx, j, partner).start()
-
-        def pair(j):
-            remote(p.at[j, 1 - core], px.at[j], sx, j, partner).wait_recv()
-            return p[j, core].astype(F32) + px[j].astype(F32)
+                n = order.index(o)
+                p[n] = partial(chip(-o)).astype(BF16).reshape(2, HALF, p.shape[3])
+                remote(p.at[n, 1 - core], px.at[n], sx, n, partner).start()
+
+        def pair(o):
+            n = order.index(o)
+            remote(p.at[n, 1 - core], px.at[n], sx, n, partner).wait_recv()
+            return p[n, core].astype(F32) + px[n].astype(F32)
 
         def first_sums(group):
             for o in group:
@@ -292,9 +298,10 @@
                     dst, target = l1.at[index], chip(lead - o)
 
                 @pl.when(j != TILES)
-                def _(j=j, dst=dst, index=index, target=target):
-                    p[j, core] = pair(j).astype(BF16)
-                    remote(p.at[j, core], dst, s1, index, at_chip(target)).start()
+                def _(o=o, dst=dst, index=index, target=target):
+                    n = order.index(o)
+                    p[n, core] = pair(o).astype(BF16)
+                    remote(p.at[n, core], dst, s1, index, at_chip(target)).start()
 
         def arrived(ref, sems, index):
             remote(ref, ref, sems, index, partner).wait_recv()
@@ -313,7 +320,7 @@
 
             @pl.when(j != TILES)
             def _(k=k, lead=lead, j=j):
-                total = pair(j)
+                total = pair(lead)
                 for slot in (2 * k, 2 * k + 1):
                     total = total + arrived(l1.at[slot], s1, slot)
                 target = j
@@ -337,7 +344,7 @@
                 remote(s.at[k - 1], l2.at[k - 1], s2, k - 1, at_chip(target)).start()
 
         def final():
-            total = pair(z)
+            total = pair(0)
             for slot in (0, 1):
                 total = total + arrived(l1.at[slot], s1, slot)
             for k in range(2 if deep else 4):
@@ -345,9 +352,12 @@
             return total
 
         def sent():
-            remote(p.at[TILES, 1 - core], px.at[TILES], sx, TILES, partner).wait_recv()
-            for j in range(TILES + 1):
-                remote(p.at[j, 1 - core], px.at[j], sx, j, partner).wait_send()
+            for n, o in enumerate(order):
+                remote(p.at[n, 1 - core], px.at[n], sx, n, partner).wait_send()
+
+                @pl.when(chip(-o) == TILES)
+                def _(n=n):
+                    remote(p.at[n, 1 - core], px.at[n], sx, n, partner).wait_recv()
             for o in range(-7, 9):
                 if o in LEADERS:
                     continue
@@ -441,9 +451,17 @@
     leads = (3, -3, 6, -6)
     others = (1, -1, 2, -2, 4, -4, 5, -5, 7, -7, 8)
 
+    def select():
+        slot = iota((ROWS * 16, 1), 0)
+        slot_token = jnp.where((slot & 15) < OWN, lax.shift_right_arithmetic(slot, 4) * OWN + (slot & 15), -1)
+        spread_s[...] = (iota((ROWS * 16, tokens), 1) == slot_token).astype(BF16)
+        compact_s[...] = (iota((tokens, ROWS * 16), 1) == token_slot).astype(BF16)
+        owner_token = jnp.where((slot & 7) < 5, lax.shift_right_arithmetic(slot, 3) * 5 + (slot & 7), -1)
+        owner_s[...] = (iota((ROWS * 16, tokens), 1) == owner_token).astype(BF16)
+
     x = x_s[...]
     forward_final, forward_sent = reduce(
-        lambda j: dot_t(x, wt_s[j]), p_s, px_s, l1_s, lx_s, s_s, l2_s, fx_sem, f1_sem, f2_sem, True
+        lambda j: dot_t(x, wt_s[j]), p_s, px_s, l1_s, lx_s, s_s, l2_s, fx_sem, f1_sem, f2_sem, False, select
     )
     h_begin, h_take, h_end, h_sent = gather(h_s, hz_sem, hc_sem)
 
@@ -458,7 +476,7 @@
         ab_s[z, core] = jnp.concatenate([up * sig * (1.0 + gate * (1.0 - sig)), silu], axis=1).astype(BF16)
 
     h_begin()
-    h_take((1, -1) + leads)
+    h_take(leads + (1, -1))
 
     @pl.when(mp == 0)
     def _():
@@ -487,6 +505,7 @@
     own_pick = ((iota((16, tokens), 1) == row * OWN + own_row) & (own_row < OWN)).astype(BF16)
     own_rows = dot(own_pick, x)
     coeff = own_unembed * gain
+    forward_sent()
     wait_bytes(all_but_one(ro_s), ro_sem.at[1, 0])
     residual = own_rows + jnp.sum(ro_s[...].astype(F32), axis=0)
     res_s[...] = residual
@@ -529,6 +548,11 @@
     def _():
         to_row(lambda o: remote(res_buf.at[row], res_buf.at[row], res_sem, 0, {"row": o}))
 
+    h_sent()
+    to_partner.wait_send()
+    wait_bytes(all_but_one(tx_buf), tx_sem.at[0, 0])
+    wait_bytes(im_buf, im_sem.at[0, 0])
+    wait_bytes(all_but_one(ro_s), ro_sem.at[0, 0])
     wait_bytes(all_but_one(sum_buf), sum_sem.at[1, 0])
     totals = jnp.sum(sum_buf[...], axis=0)
     squares = totals[0:1]
@@ -612,7 +636,7 @@
             g_s[z, core] = backward_final().astype(BF16)
 
         g_begin()
-        g_take((1, -1) + leads)
+        g_take(leads + (1, -1))
         a_end()
         g_take(others[2:])
         g_end()
@@ -640,12 +664,6 @@
         wait_bytes(rf_s, rf_sem.at[1, 0])
 
     grad_ref[...] = jnp.sum(rf_s[...], axis=0)[:5]
-    forward_sent()
-    h_sent()
-    to_partner.wait_send()
-    wait_bytes(all_but_one(tx_buf), tx_sem.at[0, 0])
-    wait_bytes(all_but_one(im_buf), im_sem.at[0, 0])
-    wait_bytes(all_but_one(ro_s), ro_sem.at[0, 0])
     wait_bytes(all_but_one(sum_buf), sum_sem.at[0, 0])
     wait_bytes(all_but_one(row_buf), row_sem.at[0, 0])
 
@@ -701,7 +719,7 @@
             half(TILES + 1, 2 * TILE, width),
             half(TILES + 1, TILE, width),
             half(ROWS, 16, width),
-            half(2 * ROWS, *image_embeds.shape),
+            half(ROWS, *image_embeds.shape),
             half(ROWS, 16, width),
             half(SEQ * 4, width),
             *tree(2 * TILE),

time: 129 us -> 129 us (level)
  no operation moved by 1% of the time
where the time goes in v3:
time: 129 us
  Pallas kernels  125 us (97%)
  between operations  2.4 us (2%)
  local copies, waits for them, and re-layouts  1.3 us (1%)
    pallas_call x1, Pallas kernels, local(): pl.pallas_call(kernel, out_shape=(jax.ShapeDtypeStruct((1, 1), F32), jax....  125 us

profile of v3, /device:TPU:1, one launch (start us, length us, event | category | flops | bytes accessed | tf_op | source)
XLA Modules:
  0.0 128.5 jit_solution(5552804422888471865)
XLA Ops:
  0.6 124.8 %dpo_block.1 = (f32[1,1]{1,0:T(1,128)}, f32[5,256]{1,0:T(8,128)}) custom-call(bf16[10,256]{1,0:T(8,128)(2,1)} %text_in.1, bf16[2,256]{1,0:T(2,128)(2,1)} %image_in.1, s32[4]{0:T(128)} %offsets_in.1, s32[4]{0:T(128)} %lengths_in.1, s32[10]{0:T(128)} %mask_in.1, bf16[1,256]{1,0:T(2,128)(2,1)} %gain_in.1, bf16[10,256]{1,0:T(8,128)(2,1)} %bitcast.8, ...), custom_call_target="tpu_custom_call" | custom-call | tf_op jit(solution)/shard_map/dpo_block/pallas_call | solution.py:704
  126.1 1.3 %copy.14 = f32[5,256]{1,0:T(8,128)} copy(f32[5,256]{1,0:T(8,128)} %get-tuple-element.9) | data formatting | bytes 10240
